TPU v7x, 128 devices: a whole 4x4x4 slice. The times are simulated.
128 devices in a mesh: req: 16 (over z_hi, y, core), head: 8 (over x, z_lo).
Axes of the slice: x: 4, y: 4, z: 4 (z_hi: 2, z_lo: 2; z = z_hi * 2 + z_lo), core: 2. Of those that a mesh axis runs over, the one named last changes fastest.
Arguments:
- tokens: bfloat16 [24576, 16384], P('req', 'head'), may hold values from -2000 to 2000
- norm_gain: bfloat16 [16384], P('head'), may hold values from 0.099609375 to 1.8984375
- kv_weight: bfloat16 [16384, 2048], P('head'), may hold values from -0.0234375 to 0.0234375
- prompt_lens: int32 [16, 32], P('req'), may hold values from 1 to 64, 1536 in all within a row
- owner_of: int32 [512, 1], P('req'), may hold values from 0 to 15; in each aligned block of 32 rows (0 to 31, 32 to 63, ...) at most 4 rows name the same one
- arr_query: bfloat16 [4, 512, 16384], P(None, 'req', 'head'), may hold values from -128 to 128
- arr_step_kv: bfloat16 [4, 512, 2048], P(None, 'req', 'head'), may hold values from -3 to 3
- prefix_kv: bfloat16 [16384, 2048], P('req', 'head'), may hold values from -6 to 6
- res_query: bfloat16 [4, 512, 16384], P(None, 'req', 'head'), may hold values from -128 to 128
- res_cache: bfloat16 [512, 512, 2048], P('req', None, 'head'), may hold values from -6 to 6
- res_step_kv: bfloat16 [4, 512, 2048], P(None, 'req', 'head'), may hold values from -3 to 3
- cache_lens: int32 [512], P('req'), may hold values from 2 to 512
Outputs:
- arr_out: float32 [4, 512, 16384], P(None, 'req', 'head')
- res_out: float32 [4, 512, 16384], P(None, 'req', 'head')
Inputs may be any that keep to these rules, and one draw needn't show every extreme that they name: `owner_of`: among the 32 requests of one index of req no owner appears more than 4 times.
All inputs are finite; a program needn't handle non-finite values.
Results may differ from a plain program's by a relative error of at most 0.012.
Values may be sent and summed in bfloat16 or wider, within the bound.
A program may use at most 128 MiB of HBM per device.

v0:
```python
from functools import reduce

import jax
import jax.numpy as jnp
from jax import lax
from jax.sharding import PartitionSpec as P

D = 16384
HD = 128
STEPS = 4
MAXLEN = 64


norm_epsilon = 1e-05


def attend(queries, key_parts):
    count_all, step_count, width_all = queries.shape
    grouped = queries.reshape(count_all, step_count, width_all // HD, HD)
    scored = []
    for key_rows, valid_mask in key_parts:
        keys_only = key_rows[..., :HD]
        if key_rows.ndim == 2:
            scores = jnp.einsum(
                "ntgd,ld->ntgl", grouped, keys_only, preferred_element_type=jnp.float32
            )
        else:
            scores = jnp.einsum(
                "ntgd,nld->ntgl", grouped, keys_only, preferred_element_type=jnp.float32
            )
        scores = scores * HD ** (-0.5)
        if valid_mask is not None:
            scores = jnp.where(valid_mask, scores, -1e30)
        scored.append(scores)
    highest = reduce(
        jnp.maximum, [jnp.max(part_scores, axis=-1, keepdims=True) for part_scores in scored]
    )
    raised = [jnp.exp(part_scores - highest) for part_scores in scored]
    totals = reduce(
        jnp.add, [jnp.sum(part_raised, axis=-1, keepdims=True) for part_raised in raised]
    )
    result = jnp.zeros(grouped.shape, jnp.float32)
    for position in range(len(key_parts)):
        values = key_parts[position][0][..., HD:]
        weights = (raised[position] / totals).astype(jnp.bfloat16)
        if values.ndim == 2:
            result = jnp.einsum(
                "ntgl,ld->ntgd", weights, values, preferred_element_type=jnp.float32
            )
        else:
            result = result + jnp.einsum(
                "ntgl,nld->ntgd", weights, values, preferred_element_type=jnp.float32
            )
    return result.reshape(count_all, step_count, width_all)


def shards(
    tokens,
    norm_gain,
    kv_weight,
    prompt_lens,
    owner_of,
    arr_query,
    arr_step_kv,
    prefix_kv,
    res_query,
    res_cache,
    res_step_kv,
    cache_lens,
):
    tok_rows = tokens.shape[0]
    pair_width = 2 * HD
    as_float = tokens.astype(jnp.float32)
    squares = jnp.sum(as_float * as_float, axis=1)
    summed_squares = lax.psum(squares, "head")
    inverse = lax.rsqrt(summed_squares / D + norm_epsilon)
    scaled = (as_float * norm_gain.astype(jnp.float32)).astype(jnp.bfloat16)
    head_count = tok_rows * lax.axis_size("head") // tok_rows
    product = jnp.dot(scaled, kv_weight, preferred_element_type=jnp.float32)
    summed = lax.psum_scatter(
        product.reshape(tok_rows, head_count, pair_width)
        .transpose(1, 0, 2)
        .reshape(head_count * tok_rows, pair_width)
        .astype(jnp.bfloat16),
        "head",
        scatter_dimension=0,
        tiled=True,
    ).astype(jnp.float32)
    new_kv = (summed * inverse[:, None]).astype(jnp.bfloat16)
    lengths = prompt_lens[0]
    request_count = lengths.shape[0]
    starts = jnp.cumsum(lengths) - lengths
    positions = jnp.arange(MAXLEN, dtype=jnp.int32)
    row_index = jnp.clip(starts[:, None] + positions[None, :], 0, tok_rows - 1)
    live_rows = positions[None, :] < lengths[:, None]
    prompt = jnp.take(new_kv, row_index.reshape(-1), axis=0).reshape(
        request_count, MAXLEN, pair_width
    )
    prompt = jnp.where(live_rows[:, :, None], prompt, jnp.zeros((), jnp.bfloat16))
    steps_valid = (jnp.arange(STEPS)[None, :] <= jnp.arange(STEPS)[:, None])[None, :, None, :]
    owners = lax.axis_size("req")
    capacity = 2 * ((request_count + owners - 1) // owners)
    owner_ids = owner_of[:, 0]
    onehot = (owner_ids[:, None] == jnp.arange(owners, dtype=jnp.int32)[None, :]).astype(jnp.int32)
    order_rank = jnp.sum((jnp.cumsum(onehot, axis=0) - onehot) * onehot, axis=1)
    slot_ids = owner_ids * capacity + order_rank
    select = (slot_ids[None, :] == jnp.arange(owners * capacity, dtype=jnp.int32)[:, None]).astype(
        jnp.bfloat16
    )
    packed_kv = (
        jnp.einsum("sn,nlc->slc", select, prompt, preferred_element_type=jnp.float32)
        .astype(jnp.bfloat16)
        .reshape(owners, capacity, MAXLEN, pair_width)
    )
    packed_query = (
        jnp.einsum("sn,tnc->stc", select, arr_query, preferred_element_type=jnp.float32)
        .astype(jnp.bfloat16)
        .reshape(owners, capacity, STEPS, arr_query.shape[2])
    )
    packed_step = (
        jnp.einsum("sn,tnc->stc", select, arr_step_kv, preferred_element_type=jnp.float32)
        .astype(jnp.bfloat16)
        .reshape(owners, capacity, STEPS, pair_width)
    )
    packed_len = (
        jnp.dot(select.astype(jnp.float32), lengths.astype(jnp.float32))
        .astype(jnp.bfloat16)
        .reshape(owners, capacity)
    )
    rows_kv = lax.all_to_all(packed_kv, "req", split_axis=0, concat_axis=0, tiled=True)
    rows_query = lax.all_to_all(packed_query, "req", split_axis=0, concat_axis=0, tiled=True)
    rows_step = lax.all_to_all(packed_step, "req", split_axis=0, concat_axis=0, tiled=True)
    rows_len = lax.all_to_all(packed_len, "req", split_axis=0, concat_axis=0, tiled=True)
    senders, item_count = rows_len.shape
    count_all = senders * item_count
    live_slots = (
        positions[None, :].astype(jnp.float32)
        < rows_len.reshape(count_all).astype(jnp.float32)[:, None]
    )
    answered = attend(
        rows_query.reshape(count_all, STEPS, rows_query.shape[3]),
        [
            (prefix_kv, None),
            (rows_kv.reshape(count_all, MAXLEN, pair_width), live_slots[:, None, None, :]),
            (rows_step.reshape(count_all, STEPS, pair_width), steps_valid),
        ],
    )
    answered = answered.reshape(senders, item_count, STEPS, rows_query.shape[3])
    replies = lax.all_to_all(
        answered.astype(jnp.bfloat16), "req", split_axis=0, concat_axis=0, tiled=True
    ).astype(answered.dtype)
    flat_replies = replies.reshape(owners * capacity, STEPS, arr_query.shape[2])
    arr_out = jnp.take(flat_replies, slot_ids, axis=0).transpose(1, 0, 2)
    cache_valid = (jnp.arange(res_cache.shape[1], dtype=jnp.int32)[None, :] < cache_lens[:, None])[
        :, None, None, :
    ]
    resident = attend(
        res_query.transpose(1, 0, 2),
        [(res_cache, cache_valid), (res_step_kv.transpose(1, 0, 2), steps_valid)],
    )
    res_out = resident.transpose(1, 0, 2)
    return (arr_out, res_out)


def solution(mesh):
    in_specs = (
        P("req", "head"),
        P("head"),
        P("head", None),
        P("req", None),
        P("req", None),
        P(None, "req", "head"),
        P(None, "req", "head"),
        P("req", "head"),
        P(None, "req", "head"),
        P("req", None, "head"),
        P(None, "req", "head"),
        P("req"),
    )
    out_specs = (P(None, "req", "head"), P(None, "req", "head"))
    return jax.shard_map(shards, mesh=mesh, in_specs=in_specs, out_specs=out_specs, check_vma=False)
```

profile of v0, /device:TPU:0, one launch (start us, length us, event | category | flops | bytes accessed | tf_op | source)
XLA Modules:
  0.0 292.6 jit_solution(13644520717596772214)
XLA Ops:
  7.2 0.7 convert_element_type.95
  8.0 17.3 %convolution_convert_fusion = bf16[1536,2048]{1,0:T(8,128)(2,1)S(1)} fusion(bf16[2048,2048]{1,0:T(8,128)(2,1)} %param.14, bf16[1536,2048]{1,0:T(8,128)(2,1)} %param.12, f32[2048]{0:T(1024)S(1)} %convert_element_type.95), kind=kOutput, calls=%fused_computation.11 | convolution fusion | flops 12897484800 | bytes 20979712 | tf_op jit(solution)/shard_map/dot_general | solution.py:79
  25.2 2.7 copy.62
  28.0 3.9 %copy.41 = bf16[8,1536,256]{2,1,0:T(8,128)(2,1)} copy(bf16[8,1536,256]{2,0,1:T(8,128)(2,1)S(1)} %bitcast.141) | data formatting | bytes 12582912 | tf_op jit(solution)/shard_map/convert_element_type | solution.py:84
  32.0 0.6 copy-done.7
  33.1 0.7 all_to_all.24
  33.8 8.0 %all-to-all-start.1 = ((bf16[16,1,4]{2,1,0:T(2,128)(2,1)}), bf16[16,1,4]{2,1,0:T(2,128)(2,1)S(1)}, u32[]{:S(2)}, u32[]{:S(2)}) async-start(bf16[16,1,4]{2,1,0:T(2,128)(2,1)} %all_to_all.24), calls=%async_computation.1 | async-start | bytes 16384 | tf_op jit(solution)/shard_map/all_to_all | solution.py:133
  42.3 4.7 %fusion.2 = f32[1536]{0:T(1024)S(1)} fusion(bf16[1536,2048]{1,0:T(8,128)(2,1)} %param.12), kind=kLoop, calls=%fused_computation.9 | loop fusion | flops 9435648 | bytes 6297600 | tf_op jit(solution)/shard_map/reduce_sum | solution.py:74
  47.0 22.0 %psum.7 = f32[1536]{0:T(1024)S(1)} all-reduce(f32[1536]{0:T(1024)S(1)} %fusion.2), channel_id=1, replica_groups=mesh['req'=16,'head'=8] {'head'}, use_global_device_ids=true, to_apply=%region_6.7 | all-reduce | flops 1536 | bytes 12288 | tf_op jit(solution)/shard_map/psum | solution.py:75
  69.5 0.5 convolution_convert_fusion.1
  70.0 5.8 %fusion.12 = (f32[32,4,16]{2,1,0:T(4,128)S(1)}, f32[32,4,16,512]{3,2,1,0:T(8,128)}) fusion(pred[32,512]{1,0:T(8,128)(4,1)S(1)} %iota_compare_fusion, bf16[32,512,256]{2,1,0:T(8,128)(2,1)} %param.21, bf16[32,4,16,128]{3,2,0,1:T(8,128)(2,1)S(1)} %bitcast.152), kind=kOutput, calls=%fused_computation.22 | convolution fusion | flops 271579136 | bytes 8937472 | tf_op jit(solution)/shard_map/ntgd,nld->ntgl/dot_general | solution.py:28
  75.9 0.7 copy.45
  76.6 7.4 %all-to-all-start.3 = ((bf16[16,4,4,256]{3,1,2,0:T(4,128)(2,1)}), bf16[16,4,4,256]{3,1,2,0:T(4,128)(2,1)S(1)}, u32[]{:S(2)}, u32[]{:S(2)}) async-start(bf16[16,4,4,256]{3,1,2,0:T(4,128)(2,1)} %copy.45), calls=%async_computation.4 | async-start | bytes 262144 | tf_op jit(solution)/shard_map/all_to_all | solution.py:132
  84.6 1.6 copy.36
  86.2 5.7 %all-to-all-done.3 = bf16[16,4,4,256]{3,1,2,0:T(4,128)(2,1)S(1)} async-done(((bf16[16,4,4,256]{3,1,2,0:T(4,128)(2,1)}), bf16[16,4,4,256]{3,1,2,0:T(4,128)(2,1)S(1)}, u32[]{:S(2)}, u32[]{:S(2)}) %all-to-all-start.3) | async-done | bytes 131104 | tf_op jit(solution)/shard_map/all_to_all | solution.py:132
  91.9 4.3 %all-to-all-start = ((bf16[16,4,4,2048]{3,1,2,0:T(4,128)(2,1)}), bf16[16,4,4,2048]{3,1,2,0:T(4,128)(2,1)}, u32[]{:S(2)}, u32[]{:S(2)}) async-start(bf16[16,4,4,2048]{3,1,2,0:T(4,128)(2,1)} %copy.36), calls=%async_computation | async-start | bytes 2097152 | tf_op jit(solution)/shard_map/all_to_all | solution.py:131
  96.3 82.1 %reduce-scatter.2.cloned.1.call-done = bf16[1536,256]{1,0:T(8,128)(2,1)} async-done(((bf16[12288,256]{1,0:T(8,128)(2,1)}), bf16[1536,256]{1,0:T(8,128)(2,1)}) %reduce-scatter.2.cloned.1.call-update) | async-done | bytes 786448 | tf_op jit(solution)/shard_map/reduce_scatter | solution.py:80
  178.4 1.4 multiply_convert_fusion
  179.8 9.1 %gather_fusion = bf16[2048,256]{1,0:T(8,128)(2,1)} fusion(bf16[1536,256]{1,0:T(8,128)(2,1)S(1)} %multiply_convert_fusion, s32[2048]{0:T(1024)S(1)} %broadcast_clamp_fusion), kind=kCustom, calls=%fused_computation | custom fusion | bytes 2105344 | tf_op jit(solution)/shard_map/jit(_take)/gather | solution.py:96
  188.8 2.5 convolution_convert_fusion.2
  191.4 2.1 reshape.260
  193.5 3.9 %copy.43 = bf16[16,4,64,256]{3,1,2,0:T(4,128)(2,1)} copy(bf16[16,4,64,256]{3,1,0,2:T(4,128)(2,1)} %reshape.260) | data formatting | bytes 4194304 | tf_op jit(solution)/shard_map/reshape | solution.py:113
  197.3 6.7 %all-to-all-start.2 = ((bf16[16,4,64,256]{3,1,2,0:T(4,128)(2,1)}), bf16[16,4,64,256]{3,1,2,0:T(4,128)(2,1)}, u32[]{:S(2)}, u32[]{:S(2)}) async-start(bf16[16,4,64,256]{3,1,2,0:T(4,128)(2,1)} %copy.43), calls=%async_computation.3 | async-start | bytes 4194304 | tf_op jit(solution)/shard_map/all_to_all | solution.py:130
  204.1 1.4 fusion.68
  205.8 3.5 %fusion.13 = f32[32,4,16]{2,1,0:T(4,128)S(1)} fusion(f32[32,4,16,512]{3,2,1,0:T(8,128)} %get-tuple-element.15, f32[32,4,16]{2,1,0:T(4,128)S(1)} %max.36, pred[32,512]{1,0:T(8,128)(4,1)S(1)} %iota_compare_fusion), kind=kLoop, calls=%fused_computation.23 | loop fusion | flops 4192256 | bytes 4227072 | tf_op jit(solution)/shard_map/reduce_sum | solution.py:40
  209.6 2.1 copy.37
  211.7 0.7 reshape_reshape.4
  212.4 2.7 fusion.67
  215.1 9.0 %multiply_reduce_fusion = (f32[64,4,16]{2,1,0:T(4,128)S(1)}, f32[64,4,16,1024]{3,2,1,0:T(8,128)}) fusion(bf16[64,4,16,128]{3,2,1,0:T(8,128)(2,1)S(1)} %reshape_reshape.4, bf16[1024,256]{1,0:T(8,128)(2,1)} %param.19), kind=kOutput, calls=%fused_computation.4 | convolution fusion | flops 1082126336 | bytes 18104320 | tf_op jit(solution)/shard_map/ntgd,ld->ntgl/dot_general | solution.py:24
  224.1 9.2 %all-to-all-done.2 = bf16[16,4,64,256]{3,1,2,0:T(4,128)(2,1)} async-done(((bf16[16,4,64,256]{3,1,2,0:T(4,128)(2,1)}), bf16[16,4,64,256]{3,1,2,0:T(4,128)(2,1)}, u32[]{:S(2)}, u32[]{:S(2)}) %all-to-all-start.2) | async-done | bytes 2097184 | tf_op jit(solution)/shard_map/all_to_all | solution.py:130
  233.4 2.0 copy.44
  235.4 0.8 fusion.19
  236.2 1.4 fusion.20
  237.6 0.5 fusion.38
  238.1 9.3 %fusion = f32[64,4,16]{2,1,0:T(4,128)S(1)} fusion(f32[64,4,16,1024]{3,2,1,0:T(8,128)} %get-tuple-element.11, f32[64,4,16]{2,1,0:T(4,128)S(1)} %bitcast.148), kind=kLoop, calls=%fused_computation.7 | loop fusion | flops 12578816 | bytes 16809984 | tf_op jit(solution)/shard_map/reduce_sum | solution.py:40
  247.5 1.3 copy-done.2
  248.8 3.8 %fusion.3 = f32[64,4,16,128]{3,2,1,0:T(8,128)S(1)} fusion(f32[64,4,16,1024]{3,2,1,0:T(8,128)S(1)} %copy-done.2, f32[64,4,16]{2,1,0:T(4,128)S(1)} %bitcast.166, f32[64,4,16]{2,1,0:T(4,128)S(1)} %bitcast.149, bf16[1024,256]{1,0:T(8,128)(2,1)S(1)} %copy-done.4), kind=kOutput, calls=%fused_computation.10 | convolution fusion | flops 1090519040 | bytes 19398656 | tf_op jit(solution)/shard_map/ntgl,ld->ntgd/dot_general | solution.py:47
  252.6 0.6 fusion.39
  253.2 1.9 add_convert_fusion
  255.1 1.1 convert_element_type.109
  256.2 4.9 %all-to-all-start.4 = ((bf16[16,4,4,2048]{3,2,1,0:T(4,128)(2,1)}), bf16[16,4,4,2048]{3,2,1,0:T(4,128)(2,1)}, u32[]{:S(2)}, u32[]{:S(2)}) async-start(bf16[16,4,4,2048]{3,2,1,0:T(4,128)(2,1)} %convert_element_type.109), calls=%async_computation.5 | async-start | bytes 2097152 | tf_op jit(solution)/shard_map/all_to_all | solution.py:149
  261.1 4.9 %fusion.6 = f32[32,4,16,128]{3,2,1,0:T(8,128)S(1)} fusion(bf16[32,512,256]{2,1,0:T(8,128)(2,1)} %param.21, f32[32,4,16,512]{3,2,1,0:T(8,128)} %get-tuple-element.15, f32[32,4,16]{2,1,0:T(4,128)S(1)} %add.125, f32[32,4,16]{2,1,0:T(4,128)S(1)} %max.36, pred[32,512]{1,0:T(8,128)(4,1)S(1)} %iota_compare_fusion), kind=kOutput, calls=%fused_computation.13 | convolution fusion | flops 273678336 | bytes 9469952 | tf_op jit(solution)/shard_map/ntgl,nld->ntgd/dot_general | solution.py:51
  266.7 1.6 copy.78
  268.3 10.8 %all-to-all-done.4 = bf16[16,4,4,2048]{3,2,1,0:T(4,128)(2,1)} async-done(((bf16[16,4,4,2048]{3,2,1,0:T(4,128)(2,1)}), bf16[16,4,4,2048]{3,2,1,0:T(4,128)(2,1)}, u32[]{:S(2)}, u32[]{:S(2)}) %all-to-all-start.4) | async-done | bytes 1048608 | tf_op jit(solution)/shard_map/all_to_all | solution.py:149
  279.1 1.4 bitcast_convert_fusion
  280.6 2.1 gather_fusion.1
  282.7 1.5 select_bitcast_fusion
  284.2 1.6 copy.51
  (60 shorter events, 3.6 us)
Async XLA Ops:
  7.2 62.3 %copy-start = (bf16[4,32,2048]{2,1,0:T(8,128)(2,1)S(1)}, bf16[4,32,2048]{2,1,0:T(8,128)(2,1)}, u32[]{:S(2)}) copy-start(bf16[4,32,2048]{2,1,0:T(8,128)(2,1)} %param.17) | copy-start | bytes 1572868
  7.2 171.2 %reduce-scatter.2.cloned.1.call-start = ((), (), s32[]{:S(2)}) async-start(), calls=%async_computation.6 | async-start | bytes 7077888 | tf_op jit(solution)/shard_map/reduce_scatter | solution.py:80
  31.9 0.7 copy-start.7
  31.9 1.0 copy-start.8
  31.9 10.3 %copy-start.3 = (bf16[4,32,2048]{2,1,0:T(8,128)(2,1)S(1)}, bf16[4,32,2048]{2,1,0:T(8,128)(2,1)}, u32[]{:S(2)}) copy-start(bf16[4,32,2048]{2,1,0:T(8,128)(2,1)} %param.20) | copy-start | bytes 1572868
  31.9 37.1 %copy-start.9 = (s32[32]{0:T(128)S(1)}, s32[32]{0:T(128)}, u32[]{:S(2)}) copy-start(s32[32]{0:T(128)} %param.23) | copy-start | bytes 388
  31.9 37.2 %copy-start.5 = (bf16[4,32,256]{2,1,0:T(8,128)(2,1)S(1)}, bf16[4,32,256]{2,1,0:T(8,128)(2,1)}, u32[]{:S(2)}) copy-start(bf16[4,32,256]{2,1,0:T(8,128)(2,1)} %param.18) | copy-start | bytes 196612
  33.8 42.8 %all-to-all-start.1 = ((bf16[16,1,4]{2,1,0:T(2,128)(2,1)}), bf16[16,1,4]{2,1,0:T(2,128)(2,1)S(1)}, u32[]{:S(2)}, u32[]{:S(2)}) async-start(bf16[16,1,4]{2,1,0:T(2,128)(2,1)} %all_to_all.24), calls=%async_computation.1 | async-start | bytes 16384 | tf_op jit(solution)/shard_map/all_to_all | solution.py:133
  75.8 10.4 %copy-start.6 = (bf16[4,32,256]{2,1,0:T(8,128)(2,1)S(1)}, bf16[4,32,256]{2,1,0:T(8,128)(2,1)}, u32[]{:S(2)}) copy-start(bf16[4,32,256]{2,1,0:T(8,128)(2,1)} %param.22) | copy-start | bytes 196612
  76.6 15.4 %all-to-all-start.3 = ((bf16[16,4,4,256]{3,1,2,0:T(4,128)(2,1)}), bf16[16,4,4,256]{3,1,2,0:T(4,128)(2,1)S(1)}, u32[]{:S(2)}, u32[]{:S(2)}) async-start(bf16[16,4,4,256]{3,1,2,0:T(4,128)(2,1)} %copy.45), calls=%async_computation.4 | async-start | bytes 262144 | tf_op jit(solution)/shard_map/all_to_all | solution.py:132
  91.9 105.4 %all-to-all-start = ((bf16[16,4,4,2048]{3,1,2,0:T(4,128)(2,1)}), bf16[16,4,4,2048]{3,1,2,0:T(4,128)(2,1)}, u32[]{:S(2)}, u32[]{:S(2)}) async-start(bf16[16,4,4,2048]{3,1,2,0:T(4,128)(2,1)} %copy.36), calls=%async_computation | async-start | bytes 2097152 | tf_op jit(solution)/shard_map/all_to_all | solution.py:131
  197.3 36.0 %all-to-all-start.2 = ((bf16[16,4,64,256]{3,1,2,0:T(4,128)(2,1)}), bf16[16,4,64,256]{3,1,2,0:T(4,128)(2,1)}, u32[]{:S(2)}, u32[]{:S(2)}) async-start(bf16[16,4,64,256]{3,1,2,0:T(4,128)(2,1)} %copy.43), calls=%async_computation.3 | async-start | bytes 4194304 | tf_op jit(solution)/shard_map/all_to_all | solution.py:130
  238.1 10.7 %copy-start.2 = (f32[64,4,16,1024]{3,2,1,0:T(8,128)S(1)}, f32[64,4,16,1024]{3,2,1,0:T(8,128)}, u32[]{:S(2)}) copy-start(f32[64,4,16,1024]{3,2,1,0:T(8,128)} %get-tuple-element.11) | copy-start | bytes 50331652
  238.1 10.7 %copy-start.4 = (bf16[1024,256]{1,0:T(8,128)(2,1)S(1)}, bf16[1024,256]{1,0:T(8,128)(2,1)}, u32[]{:S(2)}) copy-start(bf16[1024,256]{1,0:T(8,128)(2,1)} %param.19) | copy-start | bytes 1572868
  256.2 23.0 %all-to-all-start.4 = ((bf16[16,4,4,2048]{3,2,1,0:T(4,128)(2,1)}), bf16[16,4,4,2048]{3,2,1,0:T(4,128)(2,1)}, u32[]{:S(2)}, u32[]{:S(2)}) async-start(bf16[16,4,4,2048]{3,2,1,0:T(4,128)(2,1)} %convert_element_type.109), calls=%async_computation.5 | async-start | bytes 2097152 | tf_op jit(solution)/shard_map/all_to_all | solution.py:149
  268.3 17.5 %copy-start.1 = (bf16[4,32,2048]{2,1,0:T(8,128)(2,1)S(1)}, bf16[4,32,2048]{2,1,0:T(8,128)(2,1)}, u32[]{:S(2)}) copy-start(bf16[4,32,2048]{2,1,0:T(8,128)(2,1)} %param.17) | copy-start | bytes 1572868
Sparse Core Ops, SparseCore 0:
  32.0 146.2 reduce-scatter.1
where the time goes:
time: 294 us; the launch traced here: 293 us
  waiting for transfers between devices  108 us (37%)
  matrix products  52 us (18%)
  local copies, waits for them, and re-layouts  39.3 us (13%)
  starting transfers between devices  31.4 us (11%)
  other arithmetic  25.7 us (9%)
  blocking collectives  22 us (7%)
  between operations  14.5 us (5%)
    reduce_scatter x1, waiting for transfers between devices, shards(): lax.psum_scatter(product.reshape(tok_rows, head_count, pair_width).transp...  82.1 us
    psum x1, blocking collectives, shards(): summed_squares = lax.psum(squares, 'head')  22 us
    dot_general x1, matrix products, shards(): product = jnp.dot(scaled, kv_weight, preferred_element_type=jnp.float32)  17.3 us
    reduce_sum x5, other arithmetic, attend(): jnp.sum(part_raised, axis=-1, keepdims=True)  14.9 us
    all_to_all x1, waiting for transfers between devices, shards(): lax.all_to_all(answered.astype(jnp.bfloat16), 'req', split_axis=0, concat...  10.8 us
    dot_general x4, matrix products, attend(): jnp.einsum('ntgd,nld->ntgl', grouped, keys_only, preferred_element_type=j...  10.7 us
    all_to_all x1, waiting for transfers between devices, shards(): lax.all_to_all(packed_kv, 'req', split_axis=0, concat_axis=0, tiled=True)  9.23 us
    gather x1, local copies, waits for them, and re-layouts, shards(): jnp.take(new_kv, row_index.reshape(-1), axis=0)  9.06 us
  transfers between devices with their start and end apart: 6, of which 4 were waited for; matrix products, arithmetic and copies ran while one was open for 21% of the time, Pallas kernels for 0%

commit v1 on v0

v1 whole, which is shorter than its diff:
```python
import functools
import math

import jax
import jax.numpy as jnp
from jax import lax
from jax.experimental import pallas as pl
from jax.experimental.pallas import tpu as pltpu
from jax.sharding import PartitionSpec as P

D = 16384
HD = 128
PAIR = 2 * HD
STEPS = 4
GROUP = 16
ROWS = STEPS * GROUP
TOK = 1536
WIDTH = 2048
NC = 6
RB = TOK // NC
NPD = 32
OWNERS = 16
CAP = 4
PREFIX = 1024
CACHE = 512
STEP_PAD = 16
WINDOW = 80
EPS = 1e-05
LOG2E = math.log2(math.e)
SCALE = HD**-0.5 * LOG2E
MESH = pl.DeviceIdType.MESH

ORDER = ((2, 1), (1, 1), (3, 1), (2, 0), (0, 1), (1, 0), (3, 0), (0, 0))
F32 = jnp.float32
BF16 = jnp.bfloat16
NT = (((1,), (1,)), ((), ()))
TN = (((0,), (0,)), ((), ()))


def mod(a, n):
    return lax.rem(a, n)


def kernel(
    tokens, gain, weight, lens, owner, arr_query, arr_step, prefix, res_query, cache, res_step, cache_lens,
    out_res, kv, pacc, plse, aq, astep, req_slot, req_start,
    rq, rstep, done_res,
    tok, w, cach, pre, s1, s2, p20, p01, pd, p00, s1r, s2r, r2r, z2r, xr,
    ssq, slot_query,
    tok_sem, w_sem, cache_sem,
    s1_ss, s1_rs, s2_ss, s2_rs, r2_ss, r2_rs, z2_ss, z2_rs, x_ss, x_rs,
    ssq_ss, ssq_rs, pre_ss, pre_rs,
):
    r = lax.axis_index("req")
    h = lax.axis_index("head")
    x, zl = h // 2, mod(h, 2)
    zh, y, core = r // 8, mod(r // 2, 4), mod(r, 2)

    def head_at(dx, zf):
        return mod(x + dx, 4) * 2 + mod(zl + zf, 2)

    def req_at(zx, dy, cx):
        return mod(zh + zx, 2) * 8 + mod(y + dy, 4) * 2 + mod(core + cx, 2)

    def tok_copy(c):
        return pltpu.make_async_copy(tokens.at[c], tok.at[c], tok_sem.at[c])

    def w_copy(k):
        cols = pl.ds(pl.multiple_of(head_at(*ORDER[k]) * PAIR, PAIR), PAIR)
        return pltpu.make_async_copy(weight.at[:, cols], w.at[k], w_sem.at[k])

    def cache_copy(g):
        return pltpu.make_async_copy(cache.at[g], cach.at[g], cache_sem.at[g])

    tok_copy(0).start()
    w_copy(0).start()

    barrier = pltpu.get_barrier_semaphore()
    peers = [(r, mod(h + k, 8)) for k in range(1, 8)]
    peers += [(req_at(1, 0, 0), h), (req_at(0, 1, 0), h), (req_at(0, 3, 0), h), (req_at(0, 0, 1), h)]
    for peer in peers:
        pl.semaphore_signal(barrier, inc=1, device_id=peer, device_id_type=MESH)
    pl.semaphore_wait(barrier, len(peers))

    def remote(src, dst, ss, rs, device):
        return pltpu.make_async_remote_copy(
            src_ref=src, dst_ref=dst, send_sem=ss, recv_sem=rs, device_id=device, device_id_type=MESH
        )

    turn = 1 + 2 * core
    where = {"own": 0, "back": 4 - turn, "front": turn, "far": 2}
    names = [(zx, name, cx) for zx in range(2) for name in where for cx in range(2)][1:]
    held = dict(zip(names, pre))
    held[0, "own", 0] = prefix
    sends = []

    def send_prefix(name, to_name, to):
        n = len(sends)
        cp = remote(held[name], held[to_name], pre_ss.at[n], pre_rs.at[names.index(to_name)], (req_at(*to), h))
        cp.start()
        sends.append(cp)

    def wait_prefix(name):
        n = names.index(name)
        remote(held[name], held[name], pre_ss.at[0], pre_rs.at[n], (req_at(0, 0, 1), h)).wait_recv()

    def own_prefix(zx):
        send_prefix((zx, "own", 0), (zx, "back", 0), (0, turn, 0))
        send_prefix((zx, "own", 0), (zx, "front", 0), (0, 4 - turn, 0))
        send_prefix((zx, "own", 0), (zx, "own", 1), (0, 0, 1))

    def near_prefix(zx):
        wait_prefix((zx, "back", 0))
        send_prefix((zx, "back", 0), (zx, "far", 0), (0, turn, 0))
        send_prefix((zx, "back", 0), (zx, "back", 1), (0, 0, 1))
        wait_prefix((zx, "front", 0))
        send_prefix((zx, "front", 0), (zx, "front", 1), (0, 0, 1))

    def far_prefix(zx):
        wait_prefix((zx, "far", 0))
        send_prefix((zx, "far", 0), (zx, "far", 1), (0, 0, 1))

    def partner_prefix():
        wait_prefix((1, "own", 0))
        own_prefix(1)

    send_prefix((0, "own", 0), (1, "own", 0), (1, 0, 0))
    own_prefix(0)
    for c in range(1, NC):
        tok_copy(c).start()
    for k in range(1, 8):
        w_copy(k).start()
    for g in range(8):
        cache_copy(g).start()

    z_dev = (r, head_at(0, 1))

    def x_dev(step):
        return (r, mod(x + step, 4) * 2 + zl)

    def s1_copy(c):
        return remote(s1.at[c], s1r.at[c], s1_ss.at[c], s1_rs.at[c], z_dev)

    def s2_copy(d, c):
        return remote(s2.at[d, c], s2r.at[d, c], s2_ss.at[d, c], s2_rs.at[d, c], x_dev(1 + 2 * d))

    def r2_copy(c):
        return remote(p20.at[c], r2r.at[c], r2_ss.at[c], r2_rs.at[c], x_dev(1 + 2 * mod(c, 2)))

    def z2_copy(c):
        return remote(p01.at[c], z2r.at[c], z2_ss.at[c], z2_rs.at[c], z_dev)

    def x_copy(d, c):
        return remote(pd.at[d, c], xr.at[d, c], x_ss.at[d, c], x_rs.at[d, c], x_dev(1 + 2 * d))

    def project(k, c):
        return jnp.dot(tok[c], w[k], preferred_element_type=F32).astype(BF16)

    for k in range(3):
        w_copy(k).wait()

    def first(c, carry):
        tok_copy(c).wait()
        acc = []
        for b in range(4):
            rows = slice(b * (RB // 4), (b + 1) * (RB // 4))
            total = None
            for j in range(WIDTH // HD):
                cols = slice(j * HD, (j + 1) * HD)
                part = tok[c, rows, cols].astype(F32)
                square = part * part
                total = square if total is None else total + square
                tok[c, rows, cols] = (part * gain[cols].astype(F32)[None, :]).astype(BF16)
            acc.append(total)
        total = jnp.concatenate(acc, axis=0)
        s1[c] = project(0, c)
        s1_copy(c).start()
        s2[0, c] = project(1, c)
        s2_copy(0, c).start()
        s2[1, c] = project(2, c)
        s2_copy(1, c).start()
        row = lax.dot_general(
            jnp.ones((8, HD), F32), total, NT, precision=lax.Precision.HIGHEST, preferred_element_type=F32
        )
        ssq[h, c] = row[0:1, :]
        return carry

    lax.fori_loop(0, NC, first, 0)

    def ssq_copy(k):
        return remote(ssq.at[h], ssq.at[h], ssq_ss.at[k], ssq_rs.at[k], (r, mod(h + k + 1, 8)))

    for k in range(7):
        ssq_copy(k).start()

    def by_request(n, carry):
        mine = owner[n]

        def look(m, found):
            before = (m < n).astype(jnp.int32)
            return found[0] + (owner[m] == mine).astype(jnp.int32) * before, found[1] + lens[m] * before

        rank, begin = lax.fori_loop(0, NPD, look, (jnp.int32(0), jnp.int32(0)))
        req_slot[n] = mine * CAP + rank
        req_start[n] = begin
        return carry

    def by_rows(natural, rows):
        for t in range(STEPS):
            for g in range(GROUP):
                rows[:, t * GROUP + g, :] = natural[t, :, g * HD:(g + 1) * HD].astype(rows.dtype)

    def queries_by_slot():
        lax.fori_loop(0, NPD, by_request, 0)
        request = lax.broadcasted_iota(jnp.int32, (OWNERS * CAP, NPD), 1)
        held = jnp.full((OWNERS * CAP, NPD), -1, jnp.int32)
        for n in range(NPD):
            held = jnp.where(request == n, req_slot[n], held)
        slot = lax.broadcasted_iota(jnp.int32, (OWNERS * CAP, NPD), 0)
        chosen = jnp.where(held == slot, 1.0, 0.0).astype(BF16)
        for t in range(STEPS):
            for g in range(GROUP):
                part = jnp.dot(chosen, arr_query[t, :, g * HD:(g + 1) * HD], preferred_element_type=F32)
                slot_query[:, t * GROUP + g, :] = part

    def steps_by_rows(natural, rows):
        rows[...] = jnp.zeros(rows.shape, rows.dtype)
        for t in range(STEPS):
            for half in range(2):
                rows[half, :, t, :] = natural[t, :, half * HD:(half + 1) * HD].astype(rows.dtype)

    by_rows(res_query, rq)
    steps_by_rows(res_step, rstep)
    by_rows(arr_query, aq)
    steps_by_rows(arr_step, astep)

    def add(*parts):
        return functools.reduce(jnp.add, [part.astype(F32) for part in parts])

    def straight(c, carry):
        pd[0, c] = project(5, c)
        pd[1, c] = project(6, c)
        x_copy(1 - mod(c, 2), c).start()
        return carry

    def second(c, carry):
        p20[c] = project(3, c)
        p01[c] = project(4, c)
        p00[c] = project(7, c)
        return carry

    def to_far(c):
        s1_copy(c).wait_recv()
        p20[c] = add(p20[c], s1r[c]).astype(BF16)
        r2_copy(c).start()

    def to_near(c):
        d = mod(c, 2)
        r2_copy(c).wait_recv()
        pd[d, c] = add(pd[d, c], r2r[c]).astype(BF16)
        x_copy(d, c).start()

    def to_z(c, carry):
        s2_copy(0, c).wait_recv()
        s2_copy(1, c).wait_recv()
        p01[c] = add(p01[c], s2r[0, c], s2r[1, c]).astype(BF16)
        z2_copy(c).start()
        return carry

    col = lax.broadcasted_iota(jnp.int32, (ROWS, CACHE + STEP_PAD), 1)
    row_step = lax.broadcasted_iota(jnp.int32, (ROWS, CACHE + STEP_PAD), 0) // GROUP
    recent_valid = (col >= CACHE) & (col - CACHE <= row_step)

    def residents(i, carry):
        group = [i * 4 + k for k in range(4)]
        keys, values = [
            [
                jnp.concatenate([cach[i, k, :, half * HD:(half + 1) * HD], rstep[half, n].astype(BF16)], axis=0)
                for k, n in enumerate(group)
            ]
            for half in range(2)
        ]
        scores = []
        for k, n in enumerate(group):
            part = lax.dot_general(rq[n].astype(BF16), keys[k], NT, preferred_element_type=F32)
            scores.append(jnp.where((col < cache_lens[n]) | recent_valid, part, -1e30))
        scores = jnp.concatenate(scores, axis=0)
        highest = jnp.max(scores, axis=1, keepdims=True)
        raised = jnp.exp2((scores - highest) * SCALE)
        total = jnp.sum(raised, axis=1, keepdims=True)
        raised = raised.astype(BF16)
        for k, n in enumerate(group):
            rows = slice(k * ROWS, (k + 1) * ROWS)
            result = jnp.dot(raised[rows], values[k], preferred_element_type=F32)
            done_res[n] = result / total[rows]
        return carry

    def shared(zx, name, cx):
        rows = held[zx, name, cx]
        dy = where[name] if cx == 0 else mod(4 - where[name], 4)
        slots = pl.ds(pl.multiple_of(req_at(zx, dy, cx) * CAP, CAP), CAP)
        queries = slot_query[slots].reshape(CAP * ROWS, HD).astype(BF16)
        scores = lax.dot_general(queries, rows[:, :HD], NT, preferred_element_type=F32)
        highest = jnp.max(scores, axis=1, keepdims=True)
        raised = jnp.exp2((scores - highest) * SCALE)
        total = jnp.sum(raised, axis=1, keepdims=True)
        result = jnp.dot(raised.astype(BF16), rows[:, HD:], preferred_element_type=F32) / total
        level = jnp.broadcast_to(highest * SCALE + jnp.log2(total), (CAP * ROWS, HD))
        pacc[slots] = result.astype(BF16).reshape(CAP, ROWS, HD)
        plse[slots] = level.reshape(CAP, ROWS, HD)

    def shared_pair(zx, name):
        shared(zx, name, 0)
        wait_prefix((zx, name, 1))
        shared(zx, name, 1)

    def middle(c, carry):
        to_far(c)
        to_near(c - 1)
        return residents(c, carry)

    w_copy(5).wait()
    w_copy(6).wait()
    lax.fori_loop(0, NC, straight, 0)
    w_copy(3).wait()
    w_copy(4).wait()
    w_copy(7).wait()
    lax.fori_loop(0, NC, second, 0)
    queries_by_slot()
    for g in range(8):
        cache_copy(g).wait()
    to_far(0)
    residents(0, 0)
    near_prefix(0)
    lax.fori_loop(1, 3, middle, 0)
    partner_prefix()
    lax.fori_loop(3, 5, middle, 0)
    far_prefix(0)
    lax.fori_loop(5, NC, middle, 0)
    lax.fori_loop(0, NC, to_z, 0)
    to_near(NC - 1)
    lax.fori_loop(NC, NPD // 4, residents, 0)
    by_step(done_res, out_res)
    near_prefix(1)
    for name in where:
        shared_pair(0, name)
    far_prefix(1)
    for name in where:
        shared_pair(1, name)

    for k in range(7):
        ssq_copy(k).wait_recv()

    for i in range(TOK // 16, (TOK + WINDOW) // 16):
        kv[i] = jnp.zeros((16, PAIR), BF16)

    def finish(c, carry):
        z2_copy(c).wait_recv()
        x_copy(0, c).wait_recv()
        x_copy(1, c).wait_recv()
        squares = lax.dot_general(
            ssq[:, c, 0, :], jnp.ones((8, HD), F32), TN,
            precision=lax.Precision.HIGHEST, preferred_element_type=F32,
        )
        inverse = lax.rsqrt(squares * (1.0 / D) + EPS)
        total = add(p00[c], z2r[c], xr[0, c], xr[1, c])
        both = jnp.concatenate([total[:, :HD] * inverse, total[:, HD:] * inverse], axis=1)
        kv[pl.ds(pl.multiple_of(c * (RB // 16), RB // 16), RB // 16)] = both.astype(BF16).reshape(RB // 16, 16, PAIR)
        return carry

    lax.fori_loop(0, NC, finish, 0)

    def drain(c, carry):
        s1_copy(c).wait_send()
        s2_copy(0, c).wait_send()
        s2_copy(1, c).wait_send()
        r2_copy(c).wait_send()
        z2_copy(c).wait_send()
        x_copy(0, c).wait_send()
        x_copy(1, c).wait_send()
        return carry

    lax.fori_loop(0, NC, drain, 0)
    for k in range(7):
        ssq_copy(k).wait_send()
    for cp in sends:
        cp.wait_send()


def by_step(rows, natural):
    for t in range(STEPS):
        for g in range(GROUP):
            natural[t, :, g * HD:(g + 1) * HD] = rows[:, t * GROUP + g, :]


def prompts(res, kv, pacc, plse, aq, astep, req_slot, req_start, lens, out_arr, out_res, done_arr, res_sem):
    copy_res = pltpu.make_async_copy(res, out_res, res_sem)
    copy_res.start()
    width = WINDOW + STEP_PAD
    key_col = lax.broadcasted_iota(jnp.int32, (ROWS, width), 1)
    key_step = lax.broadcasted_iota(jnp.int32, (ROWS, width), 0) // GROUP
    steps_valid = (key_col >= WINDOW) & (key_col - WINDOW <= key_step)

    def arrivals(i, carry):
        group = [i * 4 + k for k in range(4)]
        scores, values = [], []
        for n in group:
            start, length = req_start[n], lens[n]
            base = lax.shift_right_logical(start, 4)
            offset = lax.bitwise_and(start, 15)
            window = [kv[base + k] for k in range(WINDOW // 16)]
            keys = jnp.concatenate([piece[:, :HD] for piece in window] + [astep[0, n].astype(BF16)], axis=0)
            values.append(jnp.concatenate([piece[:, HD:] for piece in window] + [astep[1, n].astype(BF16)], axis=0))
            part = lax.dot_general(aq[n].astype(BF16), keys, NT, preferred_element_type=F32)
            valid = ((key_col >= offset) & (key_col < offset + length)) | steps_valid
            scores.append(jnp.where(valid, part, -1e30))
        slots = [req_slot[n] for n in group]
        scores = jnp.concatenate(scores, axis=0) * SCALE
        level = jnp.concatenate([plse[slot] for slot in slots], axis=0)
        highest = jnp.maximum(jnp.max(scores, axis=1, keepdims=True), level)
        raised = jnp.exp2(scores - highest[:, :width])
        before = jnp.exp2(level - highest)
        total = jnp.sum(raised, axis=1, keepdims=True) + before
        inverse = 1.0 / total
        raised = raised.astype(BF16)
        for k, n in enumerate(group):
            rows = slice(k * ROWS, (k + 1) * ROWS)
            result = jnp.dot(raised[rows], values[k], preferred_element_type=F32)
            done_arr[n] = (result + pacc[slots[k]] * before[rows]) * inverse[rows]
        return carry

    lax.fori_loop(0, NPD // 4, arrivals, 0)
    by_step(done_arr, out_arr)
    copy_res.wait()


def fused(*operands):
    vmem = pl.BlockSpec(memory_space=pltpu.VMEM)
    smem = pl.BlockSpec(memory_space=pltpu.SMEM)
    hbm = pl.BlockSpec(memory_space=pl.ANY)
    dma = pltpu.SemaphoreType.DMA
    block = pltpu.VMEM((NC, RB, PAIR), BF16)
    pair = pltpu.VMEM((2, NC, RB, PAIR), BF16)
    by_rows = pltpu.VMEM((NPD, ROWS, HD), F32)
    steps = pltpu.VMEM((2, NPD, STEP_PAD, HD), F32)
    scratch = [
        by_rows, steps, by_rows,
        pltpu.VMEM((NC, RB, WIDTH), BF16),
        pltpu.VMEM((8, WIDTH, PAIR), BF16),
        pltpu.VMEM((8, NPD // 8, CACHE, PAIR), BF16),
        [pltpu.VMEM((PREFIX, PAIR), BF16)] * (OWNERS - 1),
        block, pair, block, block, pair, block,
        block, pair, block, block, pair,
        pltpu.VMEM((8, NC, 1, RB), F32),
        pltpu.VMEM((OWNERS * CAP, ROWS, HD), F32),
        dma((NC,)), dma((8,)), dma((8,)),
        dma((NC,)), dma((NC,)), dma((2, NC)), dma((2, NC)), dma((NC,)), dma((NC,)),
        dma((NC,)), dma((NC,)), dma((2, NC)), dma((2, NC)),
        dma((7,)), dma((7,)), dma((15,)), dma((15,)),
    ]
    out = jax.ShapeDtypeStruct((STEPS, NPD, WIDTH), F32)
    slots = (OWNERS * CAP, ROWS, HD)
    numbers = jax.ShapeDtypeStruct((NPD,), jnp.int32)
    res, *rest = pl.pallas_call(
        kernel,
        out_shape=(
            out,
            jax.ShapeDtypeStruct(((TOK + WINDOW) // 16, 16, PAIR), BF16),
            jax.ShapeDtypeStruct(slots, BF16),
            jax.ShapeDtypeStruct(slots, F32),
            jax.ShapeDtypeStruct((NPD, ROWS, HD), BF16),
            jax.ShapeDtypeStruct((2, NPD, STEP_PAD, HD), BF16),
            numbers,
            numbers,
        ),
        in_specs=[hbm, vmem, hbm, smem, smem, vmem, vmem, vmem, vmem, hbm, vmem, smem],
        out_specs=(vmem,) * 6 + (smem,) * 2,
        scratch_shapes=scratch,
        compiler_params=pltpu.CompilerParams(
            collective_id=0, has_side_effects=True, vmem_limit_bytes=63 * 2**20
        ),
        cost_estimate=pl.CostEstimate(flops=18 * 10**9, bytes_accessed=30 * 10**6, transcendentals=6 * 10**6),
        name="prefill_decode",
    )(*operands)
    return pl.pallas_call(
        prompts,
        out_shape=(out, out),
        in_specs=[hbm] + [vmem] * 5 + [smem] * 3,
        out_specs=(vmem, hbm),
        scratch_shapes=[by_rows, dma],
        compiler_params=pltpu.CompilerParams(vmem_limit_bytes=63 * 2**20),
        cost_estimate=pl.CostEstimate(flops=10**8, bytes_accessed=7 * 10**6, transcendentals=3 * 10**5),
        name="prompts",
    )(res, *rest, operands[3])


def shards(
    tokens, norm_gain, kv_weight, prompt_lens, owner_of, arr_query, arr_step_kv, prefix_kv,
    res_query, res_cache, res_step_kv, cache_lens,
):
    return fused(
        tokens.reshape(NC, RB, WIDTH), norm_gain, kv_weight, prompt_lens.reshape(NPD), owner_of.reshape(NPD), arr_query, arr_step_kv,
        prefix_kv, res_query, res_cache.reshape(8, NPD // 8, CACHE, PAIR), res_step_kv, cache_lens,
    )


def solution(mesh):
    in_specs = (
        P("req", "head"),
        P("head"),
        P("head", None),
        P("req", None),
        P("req", None),
        P(None, "req", "head"),
        P(None, "req", "head"),
        P("req", "head"),
        P(None, "req", "head"),
        P("req", None, "head"),
        P(None, "req", "head"),
        P("req"),
    )
    out_specs = (P(None, "req", "head"), P(None, "req", "head"))
    return jax.shard_map(shards, mesh=mesh, in_specs=in_specs, out_specs=out_specs, check_vma=False)
```

time: 294 us -> 124 us (0.42)
  Pallas kernels: 0 us -> 123 us
  waiting for transfers between devices: 108 us -> 0 us
  matrix products: 52 us -> 0 us
  local copies, waits for them, and re-layouts: 39.3 us -> 0 us
  starting transfers between devices: 31.4 us -> 0 us
  other arithmetic: 25.7 us -> 0 us
  blocking collectives: 22 us -> 0 us
  between operations: 14.5 us -> 0.8 us
    pallas_call x0 -> x2, Pallas kernels: none -> 123 us  [the longest x1 86.6 us: fused(): pl.pallas_call(kernel, out_shape=(out, jax.ShapeDtypeStruct(((TOK + WINDO...]
    reduce_scatter x1 -> x0, waiting for transfers between devices: 82.1 us -> none  [shards(): lax.psum_scatter(product.reshape(tok_rows, head_count, pair_width).transp...]
    dot_general x15 -> x0, matrix products: 52 us -> none  [the longest x1 17.3 us: shards(): product = jnp.dot(scaled, kv_weight, preferred_element_type=jnp.float32)]
    all_to_all x5 -> x0, starting transfers between devices: 31.4 us -> none  [the longest x1 7.98 us: shards(): lax.all_to_all(packed_len, 'req', split_axis=0, concat_axis=0, tiled=True)]
    all_to_all x5 -> x0, waiting for transfers between devices: 25.8 us -> none  [the longest x1 10.8 us: shards(): lax.all_to_all(answered.astype(jnp.bfloat16), 'req', split_axis=0, concat...]
    psum x1 -> x0, blocking collectives: 22 us -> none  [shards(): summed_squares = lax.psum(squares, 'head')]
    reduce_sum x7 -> x0, other arithmetic: 19.8 us -> none  [the longest x5 14.9 us: attend(): jnp.sum(part_raised, axis=-1, keepdims=True)]
    gather x2 -> x0, local copies, waits for them, and re-layouts: 11.1 us -> none  [the longest x1 9.06 us: shards(): jnp.take(new_kv, row_index.reshape(-1), axis=0)]
  transfers between devices with their start and end apart: 6 -> 0, of which waited for: 4 -> 0; matrix products, arithmetic and copies ran while one was open for 21% -> 0% of each run, Pallas kernels for 0% -> 0%
where the time goes in v1:
time: 124 us
  Pallas kernels  123 us (99%)
    pallas_call x1, Pallas kernels, fused(): pl.pallas_call(kernel, out_shape=(out, jax.ShapeDtypeStruct(((TOK + WINDO...  86.6 us
    pallas_call x1, Pallas kernels, fused(): pl.pallas_call(prompts, out_shape=(out, out), in_specs=[hbm] + [vmem] * 5...  36.2 us

profile of v1, /device:TPU:0, one launch (start us, length us, event | category | flops | bytes accessed | tf_op | source)
XLA Modules:
  0.0 123.6 jit_solution(7613809716530053102)
XLA Ops:
  0.6 86.6 %prefill_decode.1 = (f32[4,32,2048]{2,1,0:T(8,128)}, bf16[101,16,256]{2,1,0:T(8,128)(2,1)}, bf16[64,64,128]{2,1,0:T(8,128)(2,1)}, f32[64,64,128]{2,1,0:T(8,128)}...) custom-call(bf16[6,256,2048]{2,1,0:T(8,128)(2,1)} %bitcast.7, ...), custom_call_target="tpu_custom_call" | custom-call | flops 17999998976 | bytes 30000000 | tf_op jit(solution)/shard_map/prefill_decode/pallas_call | solution.py:464
  87.2 36.2 %prompts.1 = (f32[4,32,2048]{2,1,0:T(8,128)}, f32[4,32,2048]{2,1,0:T(8,128)}) custom-call(f32[4,32,2048]{2,1,0:T(8,128)} %get-tuple-element.10.res, bf16[101,16,256]{2,1,0:T(8,128)(2,1)} %get-tuple-element.11.kv, bf16[64,64,128]{2,1,0:T(8,128)(2,1)} %get-tuple-element.12.pacc, f32[64,64,128]{2,1,0:T(8,128)} %get-tuple-element.13.plse, ...), custom_call_target="tpu_custom_call" | custom-call | flops 100000000 | bytes 7000000 | tf_op jit(solution)/shard_map/prompts/pallas_call | solution.py:485

commit v2 on v1

--- a/solution.py
+++ b/solution.py
@@ -332,21 +332,27 @@
     to_far(0)
     residents(0, 0)
     near_prefix(0)
-    lax.fori_loop(1, 3, middle, 0)
+    lax.fori_loop(1, 2, middle, 0)
+    shared_pair(0, "own")
+    lax.fori_loop(2, 3, middle, 0)
     partner_prefix()
-    lax.fori_loop(3, 5, middle, 0)
+    shared_pair(0, "back")
+    lax.fori_loop(3, 4, middle, 0)
+    shared_pair(0, "front")
+    lax.fori_loop(4, 5, middle, 0)
     far_prefix(0)
     lax.fori_loop(5, NC, middle, 0)
     lax.fori_loop(0, NC, to_z, 0)
     to_near(NC - 1)
+    shared_pair(0, "far")
+    near_prefix(1)
+    shared_pair(1, "own")
     lax.fori_loop(NC, NPD // 4, residents, 0)
     by_step(done_res, out_res)
-    near_prefix(1)
-    for name in where:
-        shared_pair(0, name)
+    shared_pair(1, "back")
     far_prefix(1)
-    for name in where:
-        shared_pair(1, name)
+    shared_pair(1, "front")
+    shared_pair(1, "far")
 
     for k in range(7):
         ssq_copy(k).wait_recv()
@@ -393,9 +399,8 @@
             natural[t, :, g * HD:(g + 1) * HD] = rows[:, t * GROUP + g, :]
 
 
-def prompts(res, kv, pacc, plse, aq, astep, req_slot, req_start, lens, out_arr, out_res, done_arr, res_sem):
-    copy_res = pltpu.make_async_copy(res, out_res, res_sem)
-    copy_res.start()
+def prompts(res, kv, pacc, plse, aq, astep, req_slot, req_start, lens, out_arr, out_res, done_arr):
+    out_res[...] = res[...]
     width = WINDOW + STEP_PAD
     key_col = lax.broadcasted_iota(jnp.int32, (ROWS, width), 1)
     key_step = lax.broadcasted_iota(jnp.int32, (ROWS, width), 0) // GROUP
@@ -431,7 +436,6 @@
 
     lax.fori_loop(0, NPD // 4, arrivals, 0)
     by_step(done_arr, out_arr)
-    copy_res.wait()
 
 
 def fused(*operands):
@@ -485,9 +489,9 @@
     return pl.pallas_call(
         prompts,
         out_shape=(out, out),
-        in_specs=[hbm] + [vmem] * 5 + [smem] * 3,
-        out_specs=(vmem, hbm),
-        scratch_shapes=[by_rows, dma],
+        in_specs=[vmem] * 6 + [smem] * 3,
+        out_specs=(vmem, vmem),
+        scratch_shapes=[by_rows],
         compiler_params=pltpu.CompilerParams(vmem_limit_bytes=63 * 2**20),
         cost_estimate=pl.CostEstimate(flops=10**8, bytes_accessed=7 * 10**6, transcendentals=3 * 10**5),
         name="prompts",

time: 124 us -> 94.2 us (0.76)
  Pallas kernels: 123 us -> 92.5 us
    pallas_call x1, Pallas kernels: 36.2 us -> 7.46 us  [fused(): pl.pallas_call(prompts, out_shape=(out, out), in_specs=[vmem] * 6 + [smem...]
    pallas_call x1, Pallas kernels: 86.6 us -> 85 us  [fused(): pl.pallas_call(kernel, out_shape=(out, jax.ShapeDtypeStruct(((TOK + WINDO...]
where the time goes in v2:
time: 94.2 us; the launch traced here: 93.1 us
  Pallas kernels  92.5 us (98%)
    pallas_call x1, Pallas kernels, fused(): pl.pallas_call(kernel, out_shape=(out, jax.ShapeDtypeStruct(((TOK + WINDO...  85 us
    pallas_call x1, Pallas kernels, fused(): pl.pallas_call(prompts, out_shape=(out, out), in_specs=[vmem] * 6 + [smem...  7.46 us

profile of v2, /device:TPU:0, one launch (start us, length us, event | category | flops | bytes accessed | tf_op | source)
XLA Modules:
  0.0 93.1 jit_solution(14629074867413581566)
XLA Ops:
  0.6 85.0 %prefill_decode.1 = (f32[4,32,2048]{2,1,0:T(8,128)}, bf16[101,16,256]{2,1,0:T(8,128)(2,1)}, bf16[64,64,128]{2,1,0:T(8,128)(2,1)}, f32[64,64,128]{2,1,0:T(8,128)}...) custom-call(bf16[6,256,2048]{2,1,0:T(8,128)(2,1)} %bitcast.7, ...), custom_call_target="tpu_custom_call" | custom-call | flops 17999998976 | bytes 30000000 | tf_op jit(solution)/shard_map/prefill_decode/pallas_call | solution.py:468
  85.7 7.5 %prompts.1 = (f32[4,32,2048]{2,1,0:T(8,128)}, f32[4,32,2048]{2,1,0:T(8,128)}) custom-call(f32[4,32,2048]{2,1,0:T(8,128)} %get-tuple-element.10.res, bf16[101,16,256]{2,1,0:T(8,128)(2,1)} %get-tuple-element.11.kv, bf16[64,64,128]{2,1,0:T(8,128)(2,1)} %get-tuple-element.12.pacc, f32[64,64,128]{2,1,0:T(8,128)} %get-tuple-element.13.plse, ...), custom_call_target="tpu_custom_call" | custom-call | flops 100000000 | bytes 7000000 | tf_op jit(solution)/shard_map/prompts/pallas_call | solution.py:489

commit v3 on v2

--- a/solution.py
+++ b/solution.py
@@ -229,11 +229,6 @@
             for half in range(2):
                 rows[half, :, t, :] = natural[t, :, half * HD:(half + 1) * HD].astype(rows.dtype)
 
-    by_rows(res_query, rq)
-    steps_by_rows(res_step, rstep)
-    by_rows(arr_query, aq)
-    steps_by_rows(arr_step, astep)
-
     def add(*parts):
         return functools.reduce(jnp.add, [part.astype(F32) for part in parts])
 
@@ -245,6 +240,9 @@
 
     def second(c, carry):
         p20[c] = project(3, c)
+        return carry
+
+    def third(c, carry):
         p01[c] = project(4, c)
         p00[c] = project(7, c)
         return carry
@@ -323,34 +321,39 @@
     w_copy(6).wait()
     lax.fori_loop(0, NC, straight, 0)
     w_copy(3).wait()
+    lax.fori_loop(0, NC, second, 0)
+    to_far(0)
+    by_rows(res_query, rq)
+    steps_by_rows(res_step, rstep)
+    near_prefix(0)
+    for g in range(8):
+        cache_copy(g).wait()
+    lax.fori_loop(1, 2, middle, 0)
+    queries_by_slot()
+    lax.fori_loop(2, 3, middle, 0)
+    partner_prefix()
     w_copy(4).wait()
     w_copy(7).wait()
-    lax.fori_loop(0, NC, second, 0)
-    queries_by_slot()
-    for g in range(8):
-        cache_copy(g).wait()
-    to_far(0)
-    residents(0, 0)
-    near_prefix(0)
-    lax.fori_loop(1, 2, middle, 0)
+    lax.fori_loop(0, NC, third, 0)
+    lax.fori_loop(3, 4, middle, 0)
     shared_pair(0, "own")
-    lax.fori_loop(2, 3, middle, 0)
-    partner_prefix()
-    shared_pair(0, "back")
-    lax.fori_loop(3, 4, middle, 0)
-    shared_pair(0, "front")
     lax.fori_loop(4, 5, middle, 0)
     far_prefix(0)
+    shared_pair(0, "back")
     lax.fori_loop(5, NC, middle, 0)
     lax.fori_loop(0, NC, to_z, 0)
     to_near(NC - 1)
+    shared_pair(0, "front")
+    near_prefix(1)
     shared_pair(0, "far")
-    near_prefix(1)
     shared_pair(1, "own")
+    residents(0, 0)
     lax.fori_loop(NC, NPD // 4, residents, 0)
     by_step(done_res, out_res)
     shared_pair(1, "back")
     far_prefix(1)
+    by_rows(arr_query, aq)
+    steps_by_rows(arr_step, astep)
     shared_pair(1, "front")
     shared_pair(1, "far")
 

time: 94.2 us -> 98.1 us (1.041)
  Pallas kernels: 92.5 us -> 96.1 us
    pallas_call x1, Pallas kernels: 85 us -> 88.6 us  [fused(): pl.pallas_call(kernel, out_shape=(out, jax.ShapeDtypeStruct(((TOK + WINDO...]
where the time goes in v3:
time: 98.1 us; the launch traced here: 96.7 us
  Pallas kernels  96.1 us (98%)
    pallas_call x1, Pallas kernels, fused(): pl.pallas_call(kernel, out_shape=(out, jax.ShapeDtypeStruct(((TOK + WINDO...  88.6 us
    pallas_call x1, Pallas kernels, fused(): pl.pallas_call(prompts, out_shape=(out, out), in_specs=[vmem] * 6 + [smem...  7.46 us

profile of v3, /device:TPU:0, one launch (start us, length us, event | category | flops | bytes accessed | tf_op | source)
XLA Modules:
  0.0 96.7 jit_solution(7636914193165986321)
XLA Ops:
  0.6 88.6 %prefill_decode.1 = (f32[4,32,2048]{2,1,0:T(8,128)}, bf16[101,16,256]{2,1,0:T(8,128)(2,1)}, bf16[64,64,128]{2,1,0:T(8,128)(2,1)}, f32[64,64,128]{2,1,0:T(8,128)}...) custom-call(bf16[6,256,2048]{2,1,0:T(8,128)(2,1)} %bitcast.7, ...), custom_call_target="tpu_custom_call" | custom-call | flops 17999998976 | bytes 30000000 | tf_op jit(solution)/shard_map/prefill_decode/pallas_call | solution.py:471
  89.2 7.5 %prompts.1 = (f32[4,32,2048]{2,1,0:T(8,128)}, f32[4,32,2048]{2,1,0:T(8,128)}) custom-call(f32[4,32,2048]{2,1,0:T(8,128)} %get-tuple-element.10.res, bf16[101,16,256]{2,1,0:T(8,128)(2,1)} %get-tuple-element.11.kv, bf16[64,64,128]{2,1,0:T(8,128)(2,1)} %get-tuple-element.12.pacc, f32[64,64,128]{2,1,0:T(8,128)} %get-tuple-element.13.plse, ...), custom_call_target="tpu_custom_call" | custom-call | flops 100000000 | bytes 7000000 | tf_op jit(solution)/shard_map/prompts/pallas_call | solution.py:492

commit v4 on v2

--- a/solution.py
+++ b/solution.py
@@ -336,13 +336,15 @@
     shared_pair(0, "own")
     lax.fori_loop(2, 3, middle, 0)
     partner_prefix()
+    lax.fori_loop(0, 2, to_z, 0)
     shared_pair(0, "back")
     lax.fori_loop(3, 4, middle, 0)
     shared_pair(0, "front")
     lax.fori_loop(4, 5, middle, 0)
+    lax.fori_loop(2, 4, to_z, 0)
     far_prefix(0)
     lax.fori_loop(5, NC, middle, 0)
-    lax.fori_loop(0, NC, to_z, 0)
+    lax.fori_loop(4, NC, to_z, 0)
     to_near(NC - 1)
     shared_pair(0, "far")
     near_prefix(1)

time: 94.2 us -> 94.1 us (level)
  no operation moved by 1% of the time
where the time goes in v4:
time: 94.1 us; the launch traced here: 92.9 us
  Pallas kernels  92.3 us (98%)
    pallas_call x1, Pallas kernels, fused(): pl.pallas_call(kernel, out_shape=(out, jax.ShapeDtypeStruct(((TOK + WINDO...  84.8 us
    pallas_call x1, Pallas kernels, fused(): pl.pallas_call(prompts, out_shape=(out, out), in_specs=[vmem] * 6 + [smem...  7.46 us

profile of v4, /device:TPU:0, one launch (start us, length us, event | category | flops | bytes accessed | tf_op | source)
XLA Modules:
  0.0 92.9 jit_solution(8930613514515408358)
XLA Ops:
  0.6 84.8 %prefill_decode.1 = (f32[4,32,2048]{2,1,0:T(8,128)}, bf16[101,16,256]{2,1,0:T(8,128)(2,1)}, bf16[64,64,128]{2,1,0:T(8,128)(2,1)}, f32[64,64,128]{2,1,0:T(8,128)}...) custom-call(bf16[6,256,2048]{2,1,0:T(8,128)(2,1)} %bitcast.7, ...), custom_call_target="tpu_custom_call" | custom-call | flops 17999998976 | bytes 30000000 | tf_op jit(solution)/shard_map/prefill_decode/pallas_call | solution.py:470
  85.4 7.5 %prompts.1 = (f32[4,32,2048]{2,1,0:T(8,128)}, f32[4,32,2048]{2,1,0:T(8,128)}) custom-call(f32[4,32,2048]{2,1,0:T(8,128)} %get-tuple-element.10.res, bf16[101,16,256]{2,1,0:T(8,128)(2,1)} %get-tuple-element.11.kv, bf16[64,64,128]{2,1,0:T(8,128)(2,1)} %get-tuple-element.12.pacc, f32[64,64,128]{2,1,0:T(8,128)} %get-tuple-element.13.plse, ...), custom_call_target="tpu_custom_call" | custom-call | flops 100000000 | bytes 7000000 | tf_op jit(solution)/shard_map/prompts/pallas_call | solution.py:491
